TPU v7x, 256 devices: a whole 4x4x8 slice. The times are simulated.
256 devices in a mesh: scene: 8 (over y, core), blk: 32 (over x, z).
Axes of the slice: x: 4, y: 4, z: 8, core: 2. Of those that a mesh axis runs over, the one named last changes fastest.
Arguments:
- coarse_feat: bfloat16 [8, 128, 64, 256], P('scene', 'blk'), may hold values from -6 to 6
- coarse_nbr: int32 [8, 128, 4], P('scene', 'blk'), may hold values from -1 to 127, as said below
- fine_dest: int32 [8, 128], P('scene', 'blk'), may hold values from 0 to 127, as said below
- fine_nbr: int32 [8, 128, 4], P('scene', 'blk'), may hold values from -1 to 127, as said below
- skip: bfloat16 [8, 128, 512, 128], P('scene', 'blk'), may hold values from -12 to 12
- cotangent: bfloat16 [8, 128, 512, 128], P('scene', 'blk'), may hold values from -0.0078125 to 0.0078125
- w_coarse: bfloat16 [27, 256, 256], replicated, may hold values from -0.078125 to 0.078125
- w_up: bfloat16 [256, 128], replicated, may hold values from -0.375 to 0.375
- w_fine: bfloat16 [27, 128, 128], replicated, may hold values from -0.109375 to 0.109375
Outputs:
- fine_out: bfloat16 [8, 128, 512, 128], P('scene', 'blk')
- grad_fine: float32 [128, 27, 128], P('blk')
Inputs may be any that keep to these rules, and one draw needn't show every extreme that they name: `coarse_nbr`: entry k of coarse block b is the coarse index of the block beside b's face k, or -1. Neighbours are mutual, and lie on b's own device along blk or on the device just before or after it. `fine_dest`: for each scene a permutation of 0 to 127. Of the blocks that one device along blk holds in coarse order, at most 1 go to any one device along blk in fine order (fine index // 4), and that many do for some pair of devices. Entry k of fine block f is the fine index of the block beside f's face k, or -1; fine_nbr[s, fine_dest[s, b], k] = fine_dest[s, coarse_nbr[s, b, k]] where that entry is not -1, else -1. Neighbours lie on f's own device along blk or on the device just before or after it.
All inputs are finite; a program needn't handle non-finite values.
Results may differ from a plain program's by a relative error of at most 0.0058.
Values may be sent and summed in bfloat16 or wider, within the bound.
A program may use at most 64 MiB of HBM per device.

v0:
```python
import jax
import jax.numpy as jnp
from jax import lax
from jax.sharding import PartitionSpec as P

CEDGE = 4
FEDGE = 8


def with_halo(cells, sides, width):
    for axis, dim in sides:
        count = lax.axis_size(axis)
        ends = count - 1
        head = lax.slice_in_dim(cells, 0, width, axis=dim)
        tail = lax.slice_in_dim(cells, cells.shape[dim] - width, cells.shape[dim], axis=dim)
        cells = jnp.concatenate(
            [
                lax.ppermute(tail, axis, [(i, (i + 1) % count) for i in range(ends)]),
                cells,
                lax.ppermute(head, axis, [((i + 1) % count, i) for i in range(ends)]),
            ],
            axis=dim,
        )
    return cells


def upsample(block_cells, side_cells):
    block_count = block_cells.shape[0]
    channels = block_cells.shape[-1]
    cell_grid = block_cells.reshape(block_count, side_cells, side_cells, side_cells, channels)
    cell_grid = jnp.repeat(jnp.repeat(jnp.repeat(cell_grid, 2, axis=1), 2, axis=2), 2, axis=3)
    return cell_grid.reshape(block_count, 8 * side_cells**3, channels)


def facing_layers(cell_grid):
    return jnp.stack(
        [cell_grid[:, -1], cell_grid[:, 0], cell_grid[:, :, -1], cell_grid[:, :, 0]], axis=1
    )


def pad_faces(cell_grid, layers):
    padded = jnp.pad(cell_grid, ((0, 0), (1, 1), (1, 1), (1, 1), (0, 0)))
    padded = padded.at[:, 0, 1:-1, 1:-1].set(layers[:, 0])
    padded = padded.at[:, -1, 1:-1, 1:-1].set(layers[:, 1])
    padded = padded.at[:, 1:-1, 0, 1:-1].set(layers[:, 2])
    padded = padded.at[:, 1:-1, -1, 1:-1].set(layers[:, 3])
    return padded


def neighbour_layers(extended, face_table, first_index):
    row_count = extended.shape[0]
    block_count = face_table.shape[0]
    relative = face_table - first_index
    positions = jnp.arange(row_count, dtype=jnp.int32)
    chosen = []
    for face_index in range(4):
        selector = (
            (relative[:, face_index][:, None] == positions[None, :])
            & (face_table[:, face_index][:, None] >= 0)
        ).astype(jnp.bfloat16)
        flattened = extended[:, face_index].reshape(row_count, -1)
        fetched = jnp.dot(selector, flattened, preferred_element_type=jnp.float32).astype(
            jnp.bfloat16
        )
        chosen.append(fetched.reshape((block_count,) + extended.shape[2:]))
    return jnp.stack(chosen, axis=1)


def convolve(padded, weight, side_cells):
    block_count = padded.shape[0]
    channels = padded.shape[-1]
    running = None
    for off_x in range(3):
        for off_y in range(3):
            stacked = jnp.concatenate(
                [
                    padded[
                        :,
                        off_x : off_x + side_cells,
                        off_y : off_y + side_cells,
                        off_z : off_z + side_cells,
                    ]
                    for off_z in range(3)
                ],
                axis=-1,
            ).reshape(block_count * side_cells**3, 3 * channels)
            first_tap = 9 * off_x + 3 * off_y
            product = jnp.dot(
                stacked,
                weight[first_tap : first_tap + 3].reshape(3 * channels, -1),
                preferred_element_type=jnp.float32,
            )
            running = product if running is None else running + product
    return running


def silu_slope(pre_value):
    sigmoid_value = jax.nn.sigmoid(pre_value)
    return sigmoid_value * (1.0 + pre_value * (1.0 - sigmoid_value))


def body(coarse_feat, coarse_nbr, fine_dest, fine_nbr, skip, cotangent, w_coarse, w_up, w_fine):
    blocks = coarse_feat.shape[1]
    fine_chans = w_fine.shape[-1]
    peer_count = lax.axis_size("blk")
    repeats = (blocks + peer_count - 1) // peer_count
    position = lax.axis_index("blk")
    first_index = (position - 1) * blocks
    own_blocks = position * blocks + jnp.arange(blocks, dtype=jnp.int32)
    slot_index = jnp.arange(peer_count * repeats, dtype=jnp.int32)
    earlier = (
        jnp.arange(blocks, dtype=jnp.int32)[:, None] < jnp.arange(blocks, dtype=jnp.int32)[None, :]
    )
    coarse_grid = coarse_feat[0].reshape(blocks, CEDGE, CEDGE, CEDGE, -1)
    coarse_ext = with_halo(facing_layers(coarse_grid), (("blk", 0),), blocks)
    coarse_padded = pad_faces(coarse_grid, neighbour_layers(coarse_ext, coarse_nbr[0], first_index))
    coarse_act = jax.nn.silu(convolve(coarse_padded, w_coarse, CEDGE)).astype(jnp.bfloat16)
    projected = jnp.dot(coarse_act, w_up, preferred_element_type=jnp.float32).astype(jnp.bfloat16)
    projected = projected.reshape(blocks, CEDGE**3, fine_chans)
    target = fine_dest[0]
    owners = target // blocks
    same_owner = owners[:, None] == owners[None, :]
    rank = jnp.sum((same_owner & earlier).astype(jnp.int32), axis=0)
    slot_of = owners * repeats + rank
    to_slot = slot_of[None, :] == slot_index[:, None]
    labels = jnp.max(jnp.where(to_slot, target[None, :], -1), axis=1)
    weights_send = to_slot.astype(jnp.bfloat16)
    packed = jnp.dot(
        weights_send,
        upsample(projected, CEDGE).reshape(blocks, -1),
        preferred_element_type=jnp.float32,
    ).astype(jnp.bfloat16)
    arrived = lax.all_to_all(packed, "blk", split_axis=0, concat_axis=0, tiled=True)
    sources = lax.all_to_all(labels, "blk", split_axis=0, concat_axis=0, tiled=True)
    matches = (sources[None, :] == own_blocks[:, None]).astype(jnp.bfloat16)
    placed = jnp.dot(matches, arrived, preferred_element_type=jnp.float32).astype(jnp.bfloat16)
    fine_up = placed.reshape(blocks, FEDGE**3, fine_chans)
    hidden = (fine_up.astype(jnp.float32) + skip[0].astype(jnp.float32)).astype(jnp.bfloat16)
    fine_grid = hidden.reshape(blocks, FEDGE, FEDGE, FEDGE, fine_chans)
    fine_ext = with_halo(facing_layers(fine_grid), (("blk", 0),), blocks)
    fine_padded = pad_faces(fine_grid, neighbour_layers(fine_ext, fine_nbr[0], first_index))
    pre_fine = convolve(fine_padded, w_fine, FEDGE)
    outputs = [jax.nn.silu(pre_fine).astype(jnp.bfloat16).reshape(blocks, FEDGE**3, fine_chans)]
    delta_fine = (
        cotangent[0].reshape(-1, fine_chans).astype(jnp.float32) * silu_slope(pre_fine)
    ).astype(jnp.bfloat16)
    fine_out = jnp.stack(outputs)
    shard_rows = fine_chans // peer_count
    fine_padded, delta_fine = (fine_padded, delta_fine)
    tap_terms = []
    for off_x in range(3):
        for off_y in range(3):
            for off_z in range(3):
                piece = fine_padded[
                    :, off_x : off_x + FEDGE, off_y : off_y + FEDGE, off_z : off_z + FEDGE
                ].reshape(-1, fine_chans)
                tap_terms.append(
                    lax.dot_general(
                        piece,
                        delta_fine,
                        (((0,), (0,)), ((), ())),
                        preferred_element_type=jnp.float32,
                    )
                )
    running = jnp.stack(tap_terms, axis=1)
    summed = lax.psum(running, ("scene", "blk"))
    gradient = lax.dynamic_slice_in_dim(summed, position * shard_rows, shard_rows, 0)
    return (fine_out, gradient)


def solution(mesh):
    in_specs = (
        P("scene", "blk", None, None),
        P("scene", "blk", None),
        P("scene", "blk"),
        P("scene", "blk", None),
        P("scene", "blk", None, None),
        P("scene", "blk", None, None),
        P(),
        P(),
        P(),
    )
    out_specs = (P("scene", "blk", None, None), P("blk", None, None))
    return jax.shard_map(body, mesh=mesh, in_specs=in_specs, out_specs=out_specs, check_vma=False)
```

profile of v0, /device:TPU:2, one launch (start us, length us, event | category | flops | bytes accessed | tf_op | source)
XLA Modules:
  0.0 550.9 jit_solution(13759486911065288850)
XLA Ops:
  7.2 1.0 reshape_squeeze.28
  9.6 7.7 %collective-permute-start.1 = (bf16[4,4,4,4,256]{4,3,2,0,1:T(4,128)(2,1)}, bf16[4,4,4,4,256]{4,3,2,0,1:T(4,128)(2,1)}, u32[]{:S(2)}, u32[]{:S(2)}) collective-permute-start(bf16[4,4,4,4,256]{4,3,2,0,1:T(4,128)(2,1)} %pad_maximum_fusion.21), channel_id=1, source_target_pairs={{1,0},{2,1},{3,2},{4,3},{5,4},{6,5},{7,6},{8,7},{9,8},{10,9},{11,1... | collective-permute-start | bytes 393224 | tf_op jit(solution)/shard_map/ppermute | solution.py:20
  17.3 1.9 collective-permute-start
  23.4 8.6 %all-to-all-start = ((s32[32,1,1]{2,1,0:T(1,128)}), s32[32,1,1]{2,1,0:T(1,128)S(1)}, u32[]{:S(2)}, u32[]{:S(2)}) async-start(s32[32,1,1]{2,1,0:T(1,128)} %copy.71), calls=%async_computation | async-start | bytes 32768 | tf_op jit(solution)/shard_map/all_to_all | solution.py:134
  32.0 3.1 fusion.88
  36.5 1.6 fusion.53
  38.2 1.4 pad_maximum_fusion.10
  39.6 0.8 fusion.95
  40.4 1.6 reshape_squeeze.29
  42.0 1.7 convolution_convert_fusion.9
  43.7 0.8 reshape.605
  44.5 1.6 reshape_squeeze.30
  46.1 1.7 convolution_convert_fusion.8
  47.8 1.4 reshape.606
  49.3 1.6 reshape_squeeze.31
  50.8 1.7 convolution_convert_fusion.7
  52.6 1.4 reshape.607
  54.7 1.1 convolution_convert_fusion.6
  56.1 0.9 scatter.29
  57.0 0.9 scatter.30
  58.6 1.1 fusion.94
  59.8 2.3 fusion.93
  62.3 0.8 reshape.609
  63.1 1.2 pad_maximum_fusion.12
  64.3 0.8 reshape.611
  65.1 1.1 pad_maximum_fusion.13
  66.3 0.9 reshape.613
  67.2 1.2 pad_maximum_fusion.14
  68.4 0.8 reshape.615
  69.2 1.2 pad_maximum_fusion.15
  70.4 0.9 reshape.617
  71.3 1.1 pad_maximum_fusion.16
  72.5 0.8 reshape.619
  73.3 1.2 pad_maximum_fusion.17
  74.5 0.9 reshape.621
  75.4 2.0 pad_maximum_fusion.18
  77.4 1.8 reshape.623
  79.3 1.8 pad_maximum_fusion.19
  81.1 1.8 reshape.625
  82.9 1.3 fusion.96
  84.3 1.3 convolution_add_fusion.15
  89.0 3.3 fusion
  92.9 6.8 %reduce.49 = bf16[32,65536]{1,0:T(8,128)(2,1)} reduce(bf16[32,1,65536]{2,0,1:T(8,128)(2,1)} %fusion, bf16[]{:T(256)} %broadcast.212), dimensions={1}, to_apply=%copy.79.reduce_sub_computation | reduce | bytes 8388610 | tf_op jit(solution)/shard_map/all_to_all | solution.py:133
  99.7 6.6 %reshape.698 = bf16[32,2,32768]{2,1,0:T(2,128)(2,1)} reshape(bf16[32,65536]{1,0:T(8,128)(2,1)} %reduce.49) | data formatting | bytes 8388608
  106.2 10.0 %all-to-all-start.1 = ((bf16[32,2,32768]{2,1,0:T(2,128)(2,1)}), bf16[32,2,32768]{2,1,0:T(2,128)(2,1)}, u32[]{:S(2)}, u32[]{:S(2)}) async-start(bf16[32,2,32768]{2,1,0:T(2,128)(2,1)} %reshape.698), calls=%async_computation.1 | async-start | bytes 8388608 | tf_op jit(solution)/shard_map/all_to_all | solution.py:133
  117.7 91.8 %all-to-all-done.1 = bf16[32,2,32768]{2,1,0:T(2,128)(2,1)} async-done(((bf16[32,2,32768]{2,1,0:T(2,128)(2,1)}), bf16[32,2,32768]{2,1,0:T(2,128)(2,1)}, u32[]{:S(2)}, u32[]{:S(2)}) %all-to-all-start.1) | async-done | bytes 4194336 | tf_op jit(solution)/shard_map/all_to_all | solution.py:133
  209.5 20.0 %reshape.699 = bf16[32,1,65536]{2,1,0:T(2,128)(2,1)} reshape(bf16[32,2,32768]{2,1,0:T(2,128)(2,1)} %all-to-all-done.1) | data formatting | bytes 8388608
  229.5 7.9 %fusion.4 = f32[1,4,512,128]{3,1,2,0:T(4,128)S(1)} fusion(bf16[32,1,65536]{2,1,0:T(2,128)(2,1)} %reshape.699, s32[32]{0:T(128)S(1)} %reduce.16, s32[4]{0:T(128)S(1)} %iota_add_fusion), kind=kOutput, calls=%fused_computation.31 | convolution fusion | flops 17301632 | bytes 5243024 | tf_op jit(solution)/shard_map/dot_general | solution.py:136
  237.6 0.9 copy-done.14
  238.8 4.4 collective-permute-start.3
  243.2 2.0 collective-permute-start.2
  245.2 0.8 slice_reduce_fusion
  247.1 2.2 collective-permute-done.3
  249.3 5.8 %collective-permute-done.2 = bf16[4,4,8,8,128]{4,3,2,0,1:T(8,128)(2,1)S(1)} collective-permute-done((bf16[4,4,8,8,128]{4,3,2,0,1:T(8,128)(2,1)S(1)}, bf16[4,4,8,8,128]{4,3,2,0,1:T(8,128)(2,1)S(1)}, u32[]{:S(2)}, u32[]{:S(2)}) %collective-permute-start.2) | collective-permute-done | bytes 262176 | tf_op jit(solution)/shard_map/ppermute | solution.py:18
  255.5 0.9 fusion.7
  256.6 0.9 fusion.8
  257.6 0.8 fusion.9
  258.6 0.9 fusion.10
  260.5 0.9 fusion.90
  261.4 2.8 fusion.89
  271.9 1.7 fusion.38
  283.2 1.2 copy-done.2
  284.4 257.9 %all-reduce.4.cloned.1.call-done = f32[128,27,128]{2,0,1:T(8,128)} async-done(((f32[128,27,128]{2,0,1:T(8,128)}), f32[128,27,128]{2,0,1:T(8,128)}) %all-reduce.4.cloned.1.call-update) | async-done | bytes 1769488 | tf_op jit(solution)/shard_map/psum | solution.py:166
  542.3 1.5 constant_dynamic-slice_fusion
  (168 shorter events, 34.1 us)
Async XLA Ops:
  7.2 80.4 %copy-start = (bf16[256,128]{1,0:T(8,128)(2,1)S(1)}, bf16[256,128]{1,0:T(8,128)(2,1)}, u32[]{:S(2)}) copy-start(bf16[256,128]{1,0:T(8,128)(2,1)} %param.32) | copy-start | bytes 196612
  8.2 0.6 copy-start.17
  8.2 1.4 copy-start.18
  8.2 9.1 %copy-start.19 = (bf16[4,1,4,4,256]{4,3,2,0,1:T(4,128)(2,1)}, bf16[4,1,4,4,256]{4,3,2,0,1:T(4,128)(2,1)S(1)}, u32[]{:S(2)}) copy-start(bf16[4,1,4,4,256]{4,3,2,0,1:T(4,128)(2,1)S(1)} %get-tuple-element.200) | copy-start | bytes 98308
  8.3 11.0 %copy-start.20 = (bf16[4,1,4,4,256]{4,3,2,0,1:T(4,128)(2,1)}, bf16[4,1,4,4,256]{4,3,2,0,1:T(4,128)(2,1)S(1)}, u32[]{:S(2)}) copy-start(bf16[4,1,4,4,256]{4,3,2,0,1:T(4,128)(2,1)S(1)} %get-tuple-element.201) | copy-start | bytes 98308
  9.6 28.6 %collective-permute-start.1 = (bf16[4,4,4,4,256]{4,3,2,0,1:T(4,128)(2,1)}, bf16[4,4,4,4,256]{4,3,2,0,1:T(4,128)(2,1)}, u32[]{:S(2)}, u32[]{:S(2)}) collective-permute-start(bf16[4,4,4,4,256]{4,3,2,0,1:T(4,128)(2,1)} %pad_maximum_fusion.21), channel_id=1, source_target_pairs={{1,0},{2,1},{3,2},{4,3},{5,4},{6,5},{7,6},{8,7},{9,8},{10,9},{11,1... | collective-permute-start | bytes 393224 | tf_op jit(solution)/shard_map/ppermute | solution.py:20
  17.3 20.9 %collective-permute-start = (bf16[4,4,4,4,256]{4,3,2,0,1:T(4,128)(2,1)}, bf16[4,4,4,4,256]{4,3,2,0,1:T(4,128)(2,1)}, u32[]{:S(2)}, u32[]{:S(2)}) collective-permute-start(bf16[4,4,4,4,256]{4,3,2,0,1:T(4,128)(2,1)} %pad_maximum_fusion.21), channel_id=1, source_target_pairs={{0,1},{1,2},{2,3},{3,4},{4,5},{5,6},{6,7},{7,8},{8,9},{9,10},{10,1... | collective-permute-start | bytes 393224 | tf_op jit(solution)/shard_map/ppermute | solution.py:18
  21.3 0.6 copy-start.30
  23.4 82.9 %all-to-all-start = ((s32[32,1,1]{2,1,0:T(1,128)}), s32[32,1,1]{2,1,0:T(1,128)S(1)}, u32[]{:S(2)}, u32[]{:S(2)}) async-start(s32[32,1,1]{2,1,0:T(1,128)} %copy.71), calls=%async_computation | async-start | bytes 32768 | tf_op jit(solution)/shard_map/all_to_all | solution.py:134
  32.0 3.1 copy-start.22
  32.0 3.1 copy-start.23
  36.5 5.5 copy-start.32
  62.1 3.1 copy-start.13
  67.1 4.2 copy-start.12
  73.3 6.0 %copy-start.11 = (bf16[4,4,4,4,256]{4,3,2,1,0:T(4,128)(2,1)S(1)}, bf16[4,4,4,4,256]{4,3,2,1,0:T(4,128)(2,1)}, u32[]{:S(2)}) copy-start(bf16[4,4,4,4,256]{4,3,2,1,0:T(4,128)(2,1)} %get-tuple-element.166) | copy-start | bytes 393220
  75.4 7.5 %copy-start.3 = (bf16[3,256,256]{2,1,0:T(8,128)(2,1)S(1)}, bf16[3,256,256]{2,1,0:T(8,128)(2,1)}, u32[]{:S(2)}) copy-start(bf16[3,256,256]{2,1,0:T(8,128)(2,1)} %get-tuple-element.121) | copy-start | bytes 1179652
  82.9 2.7 copy-start.4
  82.9 3.0 copy-start.5
  84.2 1.9 copy-start.6
  85.6 1.0 copy-start.7
  85.9 1.0 copy-start.8
  86.2 1.1 copy-start.9
  86.6 1.0 copy-start.15
  86.6 1.1 copy-start.16
  87.7 1.3 copy-start.31
  106.2 10.0 %copy-start.24 = (s32[1,4,4]{2,1,0:T(4,128)S(1)}, s32[1,4,4]{2,1,0:T(4,128)}, u32[]{:S(2)}) copy-start(s32[1,4,4]{2,1,0:T(4,128)} %param.28) | copy-start | bytes 196
  106.2 103.3 %all-to-all-start.1 = ((bf16[32,2,32768]{2,1,0:T(2,128)(2,1)}), bf16[32,2,32768]{2,1,0:T(2,128)(2,1)}, u32[]{:S(2)}, u32[]{:S(2)}) async-start(bf16[32,2,32768]{2,1,0:T(2,128)(2,1)} %reshape.698), calls=%async_computation.1 | async-start | bytes 8388608 | tf_op jit(solution)/shard_map/all_to_all | solution.py:133
  116.2 426.1 %all-reduce.4.cloned.1.call-start = ((), (), s32[]{:S(2)}) async-start(), calls=%async_computation.2 | async-start | bytes 3538944 | tf_op jit(solution)/shard_map/psum | solution.py:166
  237.5 1.0 copy-start.14
  237.5 7.6 %copy-start.25 = (s32[4,4]{1,0:T(4,128)S(1)}, s32[4,4]{1,0:T(4,128)}, u32[]{:S(2)}) copy-start(s32[4,4]{1,0:T(4,128)} %get-tuple-element.204) | copy-start | bytes 196
  237.5 8.4 %copy-start.10 = (bf16[27,128,128]{2,1,0:T(8,128)(2,1)S(1)}, bf16[27,128,128]{2,1,0:T(8,128)(2,1)}, u32[]{:S(2)}) copy-start(bf16[27,128,128]{2,1,0:T(8,128)(2,1)} %param.33) | copy-start | bytes 2654212
  238.8 10.5 %collective-permute-start.3 = (bf16[4,4,8,8,128]{4,3,2,0,1:T(8,128)(2,1)S(1)}, bf16[4,4,8,8,128]{4,3,2,0,1:T(8,128)(2,1)S(1)}, u32[]{:S(2)}, u32[]{:S(2)}) collective-permute-start(bf16[4,4,8,8,128]{4,3,2,0,1:T(8,128)(2,1)S(1)} %pad_maximum_fusion.20), channel_id=1, source_target_pairs={{1,0},{2,1},{3,2},{4,3},{5,4},{6,5},{7,6},{8,7},{9,8},{10,9},{11,1... | collective-permute-start | bytes 786440 | tf_op jit(solution)/shard_map/ppermute | solution.py:20
  243.2 12.0 %collective-permute-start.2 = (bf16[4,4,8,8,128]{4,3,2,0,1:T(8,128)(2,1)S(1)}, bf16[4,4,8,8,128]{4,3,2,0,1:T(8,128)(2,1)S(1)}, u32[]{:S(2)}, u32[]{:S(2)}) collective-permute-start(bf16[4,4,8,8,128]{4,3,2,0,1:T(8,128)(2,1)S(1)} %pad_maximum_fusion.20), channel_id=1, source_target_pairs={{0,1},{1,2},{2,3},{3,4},{4,5},{5,6},{6,7},{7,8},{8,9},{9,10},{10,1... | collective-permute-start | bytes 786440 | tf_op jit(solution)/shard_map/ppermute | solution.py:18
  247.1 8.4 %copy-start.29 = (pred[4]{0:T(512)(128)(4,1)S(1)}, pred[4]{0:T(512)(128)(4,1)}, u32[]{:S(2)}) copy-start(pred[4]{0:T(512)(128)(4,1)} %get-tuple-element.101) | copy-start | bytes 16
  255.2 1.3 copy-start.28
  255.2 2.4 copy-start.27
  255.3 3.3 copy-start.26
  270.8 0.9 copy-start.21
  270.9 1.1 copy-start.33
  282.5 261.3 %copy-start.1 = (bf16[256,128]{1,0:T(8,128)(2,1)S(1)}, bf16[256,128]{1,0:T(8,128)(2,1)}, u32[]{:S(2)}) copy-start(bf16[256,128]{1,0:T(8,128)(2,1)} %param.32) | copy-start | bytes 196612
  283.2 1.2 copy-start.2
Sparse Core Ops, SparseCore 0:
  284.5 257.7 all-reduce.3
where the time goes:
time: 556 us; the launch traced here: 551 us
  waiting for transfers between devices  358 us (64%)
  local copies, waits for them, and re-layouts  72.8 us (13%)
  matrix products  41.5 us (7%)
  starting transfers between devices  34.6 us (6%)
  other arithmetic  28.9 us (5%)
  between operations  15.3 us (3%)
    psum x1, waiting for transfers between devices, body(): summed = lax.psum(running, ('scene', 'blk'))  258 us
    all_to_all x1, waiting for transfers between devices, body(): lax.all_to_all(packed, 'blk', split_axis=0, concat_axis=0, tiled=True)  91.8 us
    unnamed x77, local copies, waits for them, and re-layouts  31.3 us
    concatenate x18, other arithmetic, convolve(): jnp.concatenate([padded[:, off_x:off_x + side_cells, off_y:off_y + side_c...  13.2 us
    ppermute x2, starting transfers between devices, with_halo(): lax.ppermute(head, axis, [((i + 1) % count, i) for i in range(ends)])  12.1 us
  transfers between devices with their start and end apart: 7, of which 4 were waited for; matrix products, arithmetic and copies ran while one was open for 15% of the time, Pallas kernels for 0%

commit v1 on v0

--- a/solution.py
+++ b/solution.py
@@ -163,7 +163,7 @@
                     )
                 )
     running = jnp.stack(tap_terms, axis=1)
-    summed = lax.psum(running, ("scene", "blk"))
+    summed = lax.psum(lax.psum(running, "blk"), "scene")
     gradient = lax.dynamic_slice_in_dim(summed, position * shard_rows, shard_rows, 0)
     return (fine_out, gradient)
 

time: 556 us -> 517 us (0.930)
  waiting for transfers between devices: 358 us -> 319 us
    psum x1 -> x2, waiting for transfers between devices: 258 us -> 219 us  [body(): summed = lax.psum(lax.psum(running, 'blk'), 'scene')]
  transfers between devices with their start and end apart: 7 -> 8, of which waited for: 4 -> 5; matrix products, arithmetic and copies ran while one was open for 15% -> 16% of each run, Pallas kernels for 0% -> 0%
where the time goes in v1:
time: 517 us; the launch traced here: 512 us
  waiting for transfers between devices  319 us (62%)
  local copies, waits for them, and re-layouts  72.8 us (14%)
  matrix products  41.4 us (8%)
  starting transfers between devices  34.7 us (7%)
  other arithmetic  28.9 us (6%)
  between operations  15.3 us (3%)
    psum x2, waiting for transfers between devices, body(): summed = lax.psum(lax.psum(running, 'blk'), 'scene')  219 us
    all_to_all x1, waiting for transfers between devices, body(): lax.all_to_all(packed, 'blk', split_axis=0, concat_axis=0, tiled=True)  91.8 us
    unnamed x77, local copies, waits for them, and re-layouts  31.3 us
    concatenate x18, other arithmetic, convolve(): jnp.concatenate([padded[:, off_x:off_x + side_cells, off_y:off_y + side_c...  13.2 us
    ppermute x2, starting transfers between devices, with_halo(): lax.ppermute(head, axis, [((i + 1) % count, i) for i in range(ends)])  12.1 us
    dot_general x17, matrix products, convolve(): jnp.dot(stacked, weight[first_tap:first_tap + 3].reshape(3 * channels, -1...  10.6 us
  transfers between devices with their start and end apart: 8, of which 5 were waited for; matrix products, arithmetic and copies ran while one was open for 16% of the time, Pallas kernels for 0%

profile of v1, /device:TPU:2, one launch (start us, length us, event | category | flops | bytes accessed | tf_op | source)
XLA Modules:
  0.0 511.9 jit_solution(9503678835985615323)
XLA Ops:
  7.2 1.0 reshape_squeeze.28
  9.6 7.7 %collective-permute-start.1 = (bf16[4,4,4,4,256]{4,3,2,0,1:T(4,128)(2,1)}, bf16[4,4,4,4,256]{4,3,2,0,1:T(4,128)(2,1)}, u32[]{:S(2)}, u32[]{:S(2)}) collective-permute-start(bf16[4,4,4,4,256]{4,3,2,0,1:T(4,128)(2,1)} %pad_maximum_fusion.21), channel_id=1, source_target_pairs={{1,0},{2,1},{3,2},{4,3},{5,4},{6,5},{7,6},{8,7},{9,8},{10,9},{11,1... | collective-permute-start | bytes 393224 | tf_op jit(solution)/shard_map/ppermute | solution.py:20
  17.3 1.9 collective-permute-start
  23.4 8.6 %all-to-all-start = ((s32[32,1,1]{2,1,0:T(1,128)}), s32[32,1,1]{2,1,0:T(1,128)S(1)}, u32[]{:S(2)}, u32[]{:S(2)}) async-start(s32[32,1,1]{2,1,0:T(1,128)} %copy.71), calls=%async_computation | async-start | bytes 32768 | tf_op jit(solution)/shard_map/all_to_all | solution.py:134
  32.0 3.1 fusion.88
  36.5 1.6 fusion.53
  38.2 1.4 pad_maximum_fusion.10
  39.6 0.8 fusion.95
  40.4 1.6 reshape_squeeze.29
  42.0 1.7 convolution_convert_fusion.9
  44.5 1.6 reshape_squeeze.30
  46.1 1.7 convolution_convert_fusion.8
  47.8 1.4 reshape.606
  49.3 1.6 reshape_squeeze.31
  50.8 1.7 convolution_convert_fusion.7
  52.6 1.4 reshape.607
  54.7 1.1 convolution_convert_fusion.6
  56.1 0.9 scatter.29
  57.0 0.9 scatter.30
  58.6 1.1 fusion.94
  59.8 2.3 fusion.93
  62.3 0.8 reshape.609
  63.1 1.2 pad_maximum_fusion.12
  64.3 0.8 reshape.611
  65.1 1.1 pad_maximum_fusion.13
  66.3 0.9 reshape.613
  67.2 1.2 pad_maximum_fusion.14
  68.4 0.8 reshape.615
  69.2 1.2 pad_maximum_fusion.15
  70.4 0.9 reshape.617
  71.3 1.1 pad_maximum_fusion.16
  72.5 0.8 reshape.619
  73.3 1.2 pad_maximum_fusion.17
  74.5 0.9 reshape.621
  75.4 2.0 pad_maximum_fusion.18
  77.4 1.8 reshape.623
  79.3 1.8 pad_maximum_fusion.19
  81.1 1.8 reshape.625
  82.9 1.3 fusion.96
  84.3 1.3 convolution_add_fusion.15
  89.0 3.3 fusion
  92.9 6.8 %reduce.49 = bf16[32,65536]{1,0:T(8,128)(2,1)} reduce(bf16[32,1,65536]{2,0,1:T(8,128)(2,1)} %fusion, bf16[]{:T(256)} %broadcast.212), dimensions={1}, to_apply=%copy.79.reduce_sub_computation | reduce | bytes 8388610 | tf_op jit(solution)/shard_map/all_to_all | solution.py:133
  99.7 6.6 %reshape.698 = bf16[32,2,32768]{2,1,0:T(2,128)(2,1)} reshape(bf16[32,65536]{1,0:T(8,128)(2,1)} %reduce.49) | data formatting | bytes 8388608
  106.2 10.0 %all-to-all-start.1 = ((bf16[32,2,32768]{2,1,0:T(2,128)(2,1)}), bf16[32,2,32768]{2,1,0:T(2,128)(2,1)}, u32[]{:S(2)}, u32[]{:S(2)}) async-start(bf16[32,2,32768]{2,1,0:T(2,128)(2,1)} %reshape.698), calls=%async_computation.1 | async-start | bytes 8388608 | tf_op jit(solution)/shard_map/all_to_all | solution.py:133
  117.7 91.8 %all-to-all-done.1 = bf16[32,2,32768]{2,1,0:T(2,128)(2,1)} async-done(((bf16[32,2,32768]{2,1,0:T(2,128)(2,1)}), bf16[32,2,32768]{2,1,0:T(2,128)(2,1)}, u32[]{:S(2)}, u32[]{:S(2)}) %all-to-all-start.1) | async-done | bytes 4194336 | tf_op jit(solution)/shard_map/all_to_all | solution.py:133
  209.5 20.0 %reshape.699 = bf16[32,1,65536]{2,1,0:T(2,128)(2,1)} reshape(bf16[32,2,32768]{2,1,0:T(2,128)(2,1)} %all-to-all-done.1) | data formatting | bytes 8388608
  229.5 7.9 %fusion.4 = f32[1,4,512,128]{3,1,2,0:T(4,128)S(1)} fusion(bf16[32,1,65536]{2,1,0:T(2,128)(2,1)} %reshape.699, s32[32]{0:T(128)S(1)} %reduce.16, s32[4]{0:T(128)S(1)} %iota_add_fusion), kind=kOutput, calls=%fused_computation.31 | convolution fusion | flops 17301632 | bytes 5243024 | tf_op jit(solution)/shard_map/dot_general | solution.py:136
  237.6 0.9 copy-done.14
  238.8 4.4 collective-permute-start.3
  243.2 2.0 collective-permute-start.2
  245.2 0.8 slice_reduce_fusion
  247.1 2.2 collective-permute-done.3
  249.3 5.8 %collective-permute-done.2 = bf16[4,4,8,8,128]{4,3,2,0,1:T(8,128)(2,1)S(1)} collective-permute-done((bf16[4,4,8,8,128]{4,3,2,0,1:T(8,128)(2,1)S(1)}, bf16[4,4,8,8,128]{4,3,2,0,1:T(8,128)(2,1)S(1)}, u32[]{:S(2)}, u32[]{:S(2)}) %collective-permute-start.2) | collective-permute-done | bytes 262176 | tf_op jit(solution)/shard_map/ppermute | solution.py:18
  255.5 0.9 fusion.7
  256.6 0.9 fusion.8
  257.6 0.8 fusion.9
  258.6 0.9 fusion.10
  260.5 0.9 fusion.90
  261.4 2.8 fusion.89
  271.9 1.7 fusion.38
  283.2 1.2 copy-done.2
  284.4 148.2 %all-reduce.5.cloned.1.call-done = f32[128,27,128]{2,0,1:T(8,128)} async-done(((f32[128,27,128]{2,0,1:T(8,128)}), f32[128,27,128]{2,0,1:T(8,128)}) %all-reduce.5.cloned.1.call-update) | async-done | bytes 1769488 | tf_op jit(solution)/shard_map/psum | solution.py:166
  432.6 70.6 %all-reduce.7.cloned.1.call-done = f32[128,27,128]{2,0,1:T(8,128)} async-done(((f32[128,27,128]{2,0,1:T(8,128)}), f32[128,27,128]{2,0,1:T(8,128)}) %all-reduce.7.cloned.1.call-update) | async-done | bytes 1769488 | tf_op jit(solution)/shard_map/psum | solution.py:166
  503.2 1.5 constant_dynamic-slice_fusion
  (171 shorter events, 35.0 us)
Async XLA Ops:
  7.2 80.4 %copy-start = (bf16[256,128]{1,0:T(8,128)(2,1)S(1)}, bf16[256,128]{1,0:T(8,128)(2,1)}, u32[]{:S(2)}) copy-start(bf16[256,128]{1,0:T(8,128)(2,1)} %param.32) | copy-start | bytes 196612
  8.2 0.6 copy-start.17
  8.2 1.4 copy-start.18
  8.2 9.1 %copy-start.19 = (bf16[4,1,4,4,256]{4,3,2,0,1:T(4,128)(2,1)}, bf16[4,1,4,4,256]{4,3,2,0,1:T(4,128)(2,1)S(1)}, u32[]{:S(2)}) copy-start(bf16[4,1,4,4,256]{4,3,2,0,1:T(4,128)(2,1)S(1)} %get-tuple-element.200) | copy-start | bytes 98308
  8.3 11.0 %copy-start.20 = (bf16[4,1,4,4,256]{4,3,2,0,1:T(4,128)(2,1)}, bf16[4,1,4,4,256]{4,3,2,0,1:T(4,128)(2,1)S(1)}, u32[]{:S(2)}) copy-start(bf16[4,1,4,4,256]{4,3,2,0,1:T(4,128)(2,1)S(1)} %get-tuple-element.201) | copy-start | bytes 98308
  9.6 28.6 %collective-permute-start.1 = (bf16[4,4,4,4,256]{4,3,2,0,1:T(4,128)(2,1)}, bf16[4,4,4,4,256]{4,3,2,0,1:T(4,128)(2,1)}, u32[]{:S(2)}, u32[]{:S(2)}) collective-permute-start(bf16[4,4,4,4,256]{4,3,2,0,1:T(4,128)(2,1)} %pad_maximum_fusion.21), channel_id=1, source_target_pairs={{1,0},{2,1},{3,2},{4,3},{5,4},{6,5},{7,6},{8,7},{9,8},{10,9},{11,1... | collective-permute-start | bytes 393224 | tf_op jit(solution)/shard_map/ppermute | solution.py:20
  17.3 20.9 %collective-permute-start = (bf16[4,4,4,4,256]{4,3,2,0,1:T(4,128)(2,1)}, bf16[4,4,4,4,256]{4,3,2,0,1:T(4,128)(2,1)}, u32[]{:S(2)}, u32[]{:S(2)}) collective-permute-start(bf16[4,4,4,4,256]{4,3,2,0,1:T(4,128)(2,1)} %pad_maximum_fusion.21), channel_id=1, source_target_pairs={{0,1},{1,2},{2,3},{3,4},{4,5},{5,6},{6,7},{7,8},{8,9},{9,10},{10,1... | collective-permute-start | bytes 393224 | tf_op jit(solution)/shard_map/ppermute | solution.py:18
  21.3 0.6 copy-start.30
  23.4 82.9 %all-to-all-start = ((s32[32,1,1]{2,1,0:T(1,128)}), s32[32,1,1]{2,1,0:T(1,128)S(1)}, u32[]{:S(2)}, u32[]{:S(2)}) async-start(s32[32,1,1]{2,1,0:T(1,128)} %copy.71), calls=%async_computation | async-start | bytes 32768 | tf_op jit(solution)/shard_map/all_to_all | solution.py:134
  32.0 3.1 copy-start.22
  32.0 3.1 copy-start.23
  36.5 5.5 %copy-start.32 = (s32[4]{0:T(128)S(1)}, s32[4]{0:T(128)}, u32[]{:S(2)}) copy-start(s32[4]{0:T(128)} %get-tuple-element.113) | copy-start | bytes 52
  62.1 3.1 copy-start.13
  67.1 4.2 copy-start.12
  73.3 6.0 %copy-start.11 = (bf16[4,4,4,4,256]{4,3,2,1,0:T(4,128)(2,1)S(1)}, bf16[4,4,4,4,256]{4,3,2,1,0:T(4,128)(2,1)}, u32[]{:S(2)}) copy-start(bf16[4,4,4,4,256]{4,3,2,1,0:T(4,128)(2,1)} %get-tuple-element.166) | copy-start | bytes 393220
  75.4 7.5 %copy-start.3 = (bf16[3,256,256]{2,1,0:T(8,128)(2,1)S(1)}, bf16[3,256,256]{2,1,0:T(8,128)(2,1)}, u32[]{:S(2)}) copy-start(bf16[3,256,256]{2,1,0:T(8,128)(2,1)} %get-tuple-element.121) | copy-start | bytes 1179652
  82.9 2.7 copy-start.4
  82.9 3.0 copy-start.5
  84.2 1.9 copy-start.6
  85.6 1.0 copy-start.7
  85.9 1.0 copy-start.8
  86.2 1.1 copy-start.9
  86.6 1.0 copy-start.15
  86.6 1.1 copy-start.16
  87.7 1.3 copy-start.31
  106.2 10.0 %copy-start.24 = (s32[1,4,4]{2,1,0:T(4,128)S(1)}, s32[1,4,4]{2,1,0:T(4,128)}, u32[]{:S(2)}) copy-start(s32[1,4,4]{2,1,0:T(4,128)} %param.28) | copy-start | bytes 196
  106.2 103.3 %all-to-all-start.1 = ((bf16[32,2,32768]{2,1,0:T(2,128)(2,1)}), bf16[32,2,32768]{2,1,0:T(2,128)(2,1)}, u32[]{:S(2)}, u32[]{:S(2)}) async-start(bf16[32,2,32768]{2,1,0:T(2,128)(2,1)} %reshape.698), calls=%async_computation.1 | async-start | bytes 8388608 | tf_op jit(solution)/shard_map/all_to_all | solution.py:133
  116.2 316.4 %all-reduce.5.cloned.1.call-start = ((), (), s32[]{:S(2)}) async-start(), calls=%async_computation.2 | async-start | bytes 3538944 | tf_op jit(solution)/shard_map/psum | solution.py:166
  237.5 1.0 copy-start.14
  237.5 7.6 %copy-start.25 = (s32[4,4]{1,0:T(4,128)S(1)}, s32[4,4]{1,0:T(4,128)}, u32[]{:S(2)}) copy-start(s32[4,4]{1,0:T(4,128)} %get-tuple-element.204) | copy-start | bytes 196
  237.5 8.4 %copy-start.10 = (bf16[27,128,128]{2,1,0:T(8,128)(2,1)S(1)}, bf16[27,128,128]{2,1,0:T(8,128)(2,1)}, u32[]{:S(2)}) copy-start(bf16[27,128,128]{2,1,0:T(8,128)(2,1)} %param.33) | copy-start | bytes 2654212
  238.8 10.5 %collective-permute-start.3 = (bf16[4,4,8,8,128]{4,3,2,0,1:T(8,128)(2,1)S(1)}, bf16[4,4,8,8,128]{4,3,2,0,1:T(8,128)(2,1)S(1)}, u32[]{:S(2)}, u32[]{:S(2)}) collective-permute-start(bf16[4,4,8,8,128]{4,3,2,0,1:T(8,128)(2,1)S(1)} %pad_maximum_fusion.20), channel_id=1, source_target_pairs={{1,0},{2,1},{3,2},{4,3},{5,4},{6,5},{7,6},{8,7},{9,8},{10,9},{11,1... | collective-permute-start | bytes 786440 | tf_op jit(solution)/shard_map/ppermute | solution.py:20
  243.2 12.0 %collective-permute-start.2 = (bf16[4,4,8,8,128]{4,3,2,0,1:T(8,128)(2,1)S(1)}, bf16[4,4,8,8,128]{4,3,2,0,1:T(8,128)(2,1)S(1)}, u32[]{:S(2)}, u32[]{:S(2)}) collective-permute-start(bf16[4,4,8,8,128]{4,3,2,0,1:T(8,128)(2,1)S(1)} %pad_maximum_fusion.20), channel_id=1, source_target_pairs={{0,1},{1,2},{2,3},{3,4},{4,5},{5,6},{6,7},{7,8},{8,9},{9,10},{10,1... | collective-permute-start | bytes 786440 | tf_op jit(solution)/shard_map/ppermute | solution.py:18
  247.1 8.4 %copy-start.29 = (pred[4]{0:T(512)(128)(4,1)S(1)}, pred[4]{0:T(512)(128)(4,1)}, u32[]{:S(2)}) copy-start(pred[4]{0:T(512)(128)(4,1)} %get-tuple-element.101) | copy-start | bytes 16
  255.2 1.3 copy-start.28
  255.2 2.4 copy-start.27
  255.3 3.3 copy-start.26
  270.8 0.9 copy-start.21
  270.9 1.1 copy-start.33
  283.2 1.2 copy-start.2
  283.2 221.6 %copy-start.1 = (bf16[256,128]{1,0:T(8,128)(2,1)S(1)}, bf16[256,128]{1,0:T(8,128)(2,1)}, u32[]{:S(2)}) copy-start(bf16[256,128]{1,0:T(8,128)(2,1)} %param.32) | copy-start | bytes 196612
  284.4 218.8 %all-reduce.7.cloned.1.call-start = ((), (), s32[]{:S(2)}) async-start(), calls=%async_computation.3 | async-start | bytes 3538944 | tf_op jit(solution)/shard_map/psum | solution.py:166
Sparse Core Ops, SparseCore 0:
  284.5 148.0 all-reduce.4
  435.1 68.0 all-reduce.6
